TPU v7x, 128 devices: a whole 4x4x4 slice. The times are simulated.
128 devices in a mesh: depth: 2 (over core), tile: 64 (over x, y, z).
Axes of the slice: x: 4, y: 4, z: 4, core: 2. Of those that a mesh axis runs over, the one named last changes fastest.
Arguments:
- specimen: float32 [4, 2, 8192, 2048], P('depth', None, 'tile'), may hold values from -4.2 to 4.2
- scan_offsets: int32 [128, 2], P('tile'), may hold values from 0 to 7936, as said below
- probe_wave: float32 [2, 256, 256], replicated, may hold values from -4.2 to 4.2
- fresnel_phase: float32 [256, 256], replicated, may hold values from -3.140625 to 3.140625
- measured: float32 [128, 256, 256], P('tile'), may hold values from 0 to 3
Outputs:
- specimen_gradient: float32 [4, 2, 8192, 2048], P('depth', None, 'tile')
Inputs may be any that keep to these rules, and one draw needn't show every extreme that they name: `scan_offsets`: A position held by tile index d (positions d * 2 to (d + 1) * 2 - 1) has its top row between max(0, (d - 1) * 128) and min(d * 128, 7936), and its left column at most 1792.
All inputs are finite; a program needn't handle non-finite values.
Results may differ from a plain program's by a relative error of at most 0.0003.
Values sent between devices are 32-bit elements; how exact they have to be, the bound alone decides.
A program may use at most 128 MiB of HBM per device.

v0:
```python
import functools

import jax
import jax.numpy as jnp
import ml_dtypes
import numpy as np
from jax import lax
from jax.experimental import pallas as pl
from jax.experimental.pallas import tpu as pltpu
from jax.sharding import PartitionSpec as P

MESH = pl.DeviceIdType.MESH
F32 = jnp.float32
BF16 = jnp.bfloat16
HALF = 128
FULL = 256


def halves(matrix):
    high = matrix.astype(ml_dtypes.bfloat16)
    low = (matrix - high.astype(np.float64)).astype(ml_dtypes.bfloat16)
    return high, low


def dft_tables():
    n = np.arange(HALF)
    tables = []
    for parity in (0, 1):
        angle = 2.0 * np.pi * ((n[:, None] * (2 * n[None, :] + parity)) % FULL) / FULL
        cosine, sine = np.cos(angle) / 16.0, np.sin(angle) / 16.0
        right = np.block([[cosine, -sine], [sine, cosine]])
        tables.append(right)
    parts = [halves(m) for right in tables for m in (right, right.T)]
    return np.stack([np.stack(p) for p in parts])


def order_tables():
    order = np.concatenate([np.arange(0, FULL, 2), np.arange(1, FULL, 2)])
    right = np.zeros((FULL, FULL), np.float32)
    right[order, np.arange(FULL)] = 1.0
    return np.stack([right, right.T]).astype(ml_dtypes.bfloat16)


def dot(a, b):
    return jnp.dot(a, b, preferred_element_type=F32)


def two_parts(x):
    high = x.astype(BF16)
    low = (x - high.astype(F32)).astype(BF16)
    return high, low


def exact_right(x, ones):
    high = x.astype(BF16)
    rest = x - high.astype(F32)
    middle = rest.astype(BF16)
    low = (rest - middle.astype(F32)).astype(BF16)
    return (dot(high, ones) + dot(middle, ones)) + dot(low, ones)


def exact_left(ones, x):
    high = x.astype(BF16)
    rest = x - high.astype(F32)
    middle = rest.astype(BF16)
    low = (rest - middle.astype(F32)).astype(BF16)
    return (dot(ones, high) + dot(ones, middle)) + dot(ones, low)


def times_right(x, table):
    high, low = two_parts(x)
    return dot(high, table[0]) + (dot(low, table[0]) + dot(high, table[1]))


def times_left(table, x):
    high, low = two_parts(x)
    return dot(table[0], high) + (dot(table[0], low) + dot(table[1], high))


EVEN, EVEN_T, ODD, ODD_T = range(4)


def forward_transform(x_ref, z_ref, tab):
    re, im = x_ref[0], x_ref[1]
    even = jnp.concatenate([re[:, :HALF] + re[:, HALF:], im[:, :HALF] + im[:, HALF:]], 1)
    odd = jnp.concatenate([re[:, :HALF] - re[:, HALF:], im[:, :HALF] - im[:, HALF:]], 1)
    ye = times_right(even, tab.at[EVEN])
    yo = times_right(odd, tab.at[ODD])
    re = jnp.concatenate([ye[:, :HALF], yo[:, :HALF]], 1)
    im = jnp.concatenate([ye[:, HALF:], yo[:, HALF:]], 1)
    z_ref[0] = times_left(tab.at[EVEN_T], jnp.concatenate([re[:HALF] + re[HALF:], im[:HALF] + im[HALF:]], 0))
    z_ref[1] = times_left(tab.at[ODD_T], jnp.concatenate([re[:HALF] - re[HALF:], im[:HALF] - im[HALF:]], 0))


def inverse_transform(z_ref, out, tab):
    a = times_left(tab.at[EVEN], z_ref[0])
    b = times_left(tab.at[ODD], z_ref[1])
    total, rest = a + b, a - b
    re = jnp.concatenate([total[:HALF], rest[:HALF]], 0)
    im = jnp.concatenate([total[HALF:], rest[HALF:]], 0)
    a = times_right(jnp.concatenate([re[:, :HALF], im[:, :HALF]], 1), tab.at[EVEN_T])
    b = times_right(jnp.concatenate([re[:, HALF:], im[:, HALF:]], 1), tab.at[ODD_T])
    total, rest = a + b, a - b
    out[0] = jnp.concatenate([total[:, :HALF], rest[:, :HALF]], 1)
    out[1] = jnp.concatenate([total[:, HALF:], rest[:, HALF:]], 1)


def column_block(column, width):
    block = jnp.minimum(lax.shift_right_logical(column, 7), width // HALF - 3)
    return block, column - block * HALF


def take_window(spec, layer, component, column, width):
    block, shift = column_block(column, width)
    lane = lax.broadcasted_iota(jnp.int32, (HALF, HALF), 1)
    mixed = jnp.where(lane >= shift, spec[layer, component, block], spec[layer, component, block + 2])
    return mixed, spec[layer, component, block + 1]


def main_kernel(
    tiles, width,
    offs, spec_hbm, probe_hbm, phase_hbm, meas_hbm, tab_hbm, perm_hbm,
    grads, offs_out,
    spec, probe, phase, meas, tab, perm,
    staged, near, own_staged, own, patch, field, x_buf, z_buf, kern, update, offs_land,
    block_sem, load_sem, off_send, off_recv, in_send, in_recv, sib_send, sib_recv,
    out_send, out_recv, mid_send, mid_recv, mid_local,
):
    me = lax.axis_index("tile")
    core = lax.axis_index("depth")
    other = 1 - core
    has_above = me > 0
    has_below = me < tiles - 1
    above = jnp.maximum(me - 1, 0)
    below = jnp.minimum(me + 1, tiles - 1)

    barrier = pltpu.get_barrier_semaphore()
    pl.semaphore_signal(barrier, inc=1, device_id=(other, me), device_id_type=MESH)

    @pl.when(has_above)
    def _():
        for d in (0, 1):
            pl.semaphore_signal(barrier, inc=1, device_id=(d, above), device_id_type=MESH)

    @pl.when(has_below)
    def _():
        for d in (0, 1):
            pl.semaphore_signal(barrier, inc=1, device_id=(d, below), device_id_type=MESH)

    blocks = width // HALF

    def block_copy(b):
        return pltpu.make_async_copy(
            spec_hbm.at[:, :, :, pl.ds(b * HALF, HALF)], spec.at[:, :, b], block_sem.at[b]
        )

    loads = [
        pltpu.make_async_copy(tab_hbm, tab, load_sem.at[0]),
        pltpu.make_async_copy(perm_hbm, perm, load_sem.at[1]),
        pltpu.make_async_copy(probe_hbm, probe, load_sem.at[2]),
        pltpu.make_async_copy(phase_hbm, phase, load_sem.at[3]),
        pltpu.make_async_copy(meas_hbm.at[core], meas, load_sem.at[4]),
    ]
    for b in range(blocks):
        block_copy(b).start()
    for copy in loads:
        copy.start()
    pl.semaphore_wait(barrier, 1 + 2 * has_above.astype(jnp.int32) + 2 * has_below.astype(jnp.int32))

    def offsets_copy(side):
        return pltpu.make_async_remote_copy(
            src_ref=offs, dst_ref=offs_land.at[1 - side], send_sem=off_send.at[side], recv_sem=off_recv.at[1 - side],
            device_id=(core, above if side == 0 else below), device_id_type=MESH,
        )

    sides = ((0, has_above), (1, has_below))
    for side, there in sides:
        pl.when(there)(offsets_copy(side).start)

    for b in range(blocks):
        block_copy(b).wait()
    for layer in (0, 1):
        for c in (0, 1):
            mixed, pure = take_window(spec, layer, c, offs[other, 1], width)
            own_staged[layer, c, :, :HALF] = mixed
            own_staged[layer, c, :, HALF:] = pure

    def sibling_copy(layer):
        return pltpu.make_async_remote_copy(
            src_ref=own_staged.at[layer], dst_ref=own.at[2 * core + layer], send_sem=sib_send.at[layer],
            recv_sem=sib_recv.at[layer], device_id=(other, me), device_id_type=MESH,
        )

    for layer in (0, 1):
        sibling_copy(layer).start()
    for layer in (0, 1):
        for c in (0, 1):
            mixed, pure = take_window(spec, layer, c, offs[core, 1], width)
            own[2 * core + layer, c, :, :HALF] = mixed
            own[2 * core + layer, c, :, HALF:] = pure

    def window_copy(position, layer, side):
        return pltpu.make_async_remote_copy(
            src_ref=staged.at[side, position, layer], dst_ref=near.at[1 - side, 2 * core + layer],
            send_sem=in_send.at[side, position, layer], recv_sem=in_recv.at[1 - side, 2 * core + layer],
            device_id=(position, above if side == 0 else below), device_id_type=MESH,
        )

    for side, there in sides:
        @pl.when(there)
        def _(side=side):
            pltpu.make_async_remote_copy(
                src_ref=offs, dst_ref=offs_land.at[side], send_sem=off_send.at[side], recv_sem=off_recv.at[side],
                device_id=(core, above if side == 0 else below), device_id_type=MESH,
            ).wait_recv()

    for position in (0, 1):
        for layer in (0, 1):
            for side, there in sides:
                @pl.when(there)
                def _(position=position, layer=layer, side=side):
                    for c in (0, 1):
                        mixed, pure = take_window(spec, layer, c, offs_land[side, position, 1], width)
                        staged[side, position, layer, c, :, :HALF] = mixed
                        staged[side, position, layer, c, :, HALF:] = pure
                    window_copy(position, layer, side).start()

    for side, there in sides:
        for position in (0, 1):
            first = offs_land[side, position, 0] - (me - 2 + 2 * side) * HALF
            offs_out[side, position, 0] = jnp.where(there, first, HALF * side)
            offs_out[side, position, 1] = jnp.where(there, offs_land[side, position, 1], 0)

    first = offs[core, 0] - (me - 1) * HALF
    unused, shift = column_block(offs[core, 1], width)
    for copy in loads:
        copy.wait()
    phases = exact_right(exact_left(perm[1], phase[...]), perm[0])
    kern[0] = jnp.cos(phases)
    kern[1] = jnp.sin(phases)
    meas[...] = exact_right(exact_left(perm[1], meas[...]), perm[0])
    rows = lax.broadcasted_iota(jnp.int32, (FULL, FULL), 0)
    cols = lax.broadcasted_iota(jnp.int32, (FULL, FULL), 1)
    turn = jnp.where(((cols + first) & (FULL - 1)) == rows, 1.0, 0.0).astype(BF16)
    slide = jnp.where(((rows + shift) & (FULL - 1)) == cols, 1.0, 0.0).astype(BF16)
    for c in (0, 1):
        field[0, c] = exact_right(exact_left(turn, probe[c]), slide)

    for layer in (0, 1):
        pltpu.make_async_remote_copy(
            src_ref=own_staged.at[layer], dst_ref=own.at[2 * other + layer], send_sem=sib_send.at[layer],
            recv_sem=sib_recv.at[layer], device_id=(other, me), device_id_type=MESH,
        ).wait_recv()

    half_rows = lax.broadcasted_iota(jnp.int32, (HALF, FULL), 0)

    def update_copy(s, side):
        target = s // 2
        return pltpu.make_async_remote_copy(
            src_ref=update.at[s, :, pl.ds(0, HALF)], dst_ref=grads.at[s - 2 * target, 2 * (1 - side) + core],
            send_sem=out_send.at[side, s], recv_sem=out_recv.at[s - 2 * target, 2 * (1 - side) + core],
            device_id=(target, above if side == 0 else below), device_id_type=MESH,
        )

    def middle_copy(layer):
        return pltpu.make_async_remote_copy(
            src_ref=update.at[2 * other + layer, :, pl.ds(HALF, HALF)], dst_ref=grads.at[layer, 4 + core],
            send_sem=mid_send.at[layer], recv_sem=mid_recv.at[layer], device_id=(other, me), device_id_type=MESH,
        )

    def middle_local(layer):
        return pltpu.make_async_copy(
            update.at[2 * core + layer, :, pl.ds(HALF, HALF)], grads.at[layer, 4 + core], mid_local.at[layer]
        )

    def step(i, carry):
        @pl.when(i <= 3)
        def _():
            for side, there in sides:
                @pl.when(there)
                def _(side=side):
                    pltpu.make_async_remote_copy(
                        src_ref=staged.at[side, 0, 0], dst_ref=near.at[side, i], send_sem=in_send.at[side, 0, 0],
                        recv_sem=in_recv.at[side, i], device_id=(core, above if side == 0 else below),
                        device_id_type=MESH,
                    ).wait_recv()
            top = [jnp.where(half_rows >= first, near[0, i, c], near[1, i, c]) for c in (0, 1)]
            bottom = [own[i, c] for c in (0, 1)]
            for c in (0, 1):
                patch[i, c, :HALF] = top[c]
                patch[i, c, HALF:] = bottom[c]
            for part, (pr, pi) in enumerate((top, bottom)):
                span = pl.ds(part * HALF, HALF)
                wr, wi = field[i, 0, span], field[i, 1, span]
                x_buf[0, span] = wr * pr - wi * pi
                x_buf[1, span] = wr * pi + wi * pr

        @pl.when(i > 3)
        def _():
            pr, pi = patch[7 - i, 0], patch[7 - i, 1]
            ar, ai = field[i, 0], field[i, 1]
            x_buf[0] = pr * ar + pi * ai
            x_buf[1] = pr * ai - pi * ar

        forward_transform(x_buf, z_buf, tab)

        @pl.when(i == 3)
        def _():
            for parity in (0, 1):
                zr, zi = z_buf[parity, :HALF], z_buf[parity, HALF:]
                e = 2.0 * (zr * zr + zi * zi - meas[parity * HALF : (parity + 1) * HALF])
                z_buf[parity, :HALF] = e * zr
                z_buf[parity, HALF:] = e * zi

        @pl.when(i != 3)
        def _():
            sign = jnp.where(i < 3, 1.0, -1.0)
            for parity in (0, 1):
                span = slice(parity * HALF, (parity + 1) * HALF)
                zr, zi = z_buf[parity, :HALF], z_buf[parity, HALF:]
                kr, ki = kern[0, span], sign * kern[1, span]
                z_buf[parity, :HALF] = kr * zr - ki * zi
                z_buf[parity, HALF:] = kr * zi + ki * zr

        inverse_transform(z_buf, field.at[i + 1], tab)

        @pl.when(i >= 3)
        def _():
            s = 6 - i
            wr, wi = field[s, 0], field[s, 1]
            ar, ai = field[i + 1, 0], field[i + 1, 1]
            update[s, 0] = wr * ar + wi * ai
            update[s, 1] = wr * ai - wi * ar
            for side, there in sides:
                @pl.when(there)
                def _(side=side):
                    update_copy(s, side).start()
            for layer in (0, 1):
                pl.when(s == 2 * other + layer)(middle_copy(layer).start)
                pl.when(s == 2 * core + layer)(middle_local(layer).start)

        return carry

    lax.fori_loop(0, 7, step, 0)

    for layer in (0, 1):
        middle_local(layer).wait()
        middle_copy(layer).wait_send()
        pltpu.make_async_remote_copy(
            src_ref=update.at[0, :, pl.ds(HALF, HALF)], dst_ref=grads.at[layer, 4 + other],
            send_sem=mid_send.at[layer], recv_sem=mid_recv.at[layer], device_id=(other, me), device_id_type=MESH,
        ).wait_recv()
        sibling_copy(layer).wait_send()
    for side, there in sides:
        @pl.when(there)
        def _(side=side):
            offsets_copy(side).wait_send()
            for position in (0, 1):
                for layer in (0, 1):
                    window_copy(position, layer, side).wait_send()
            for s in range(4):
                update_copy(s, side).wait_send()
            for layer in (0, 1):
                for position in (0, 1):
                    pltpu.make_async_remote_copy(
                        src_ref=update.at[0, :, pl.ds(0, HALF)], dst_ref=grads.at[layer, 2 * side + position],
                        send_sem=out_send.at[side, 0], recv_sem=out_recv.at[layer, 2 * side + position],
                        device_id=(core, above if side == 0 else below), device_id_type=MESH,
                    ).wait_recv()


def place_kernel(width, offs, near_offs, grads, out):
    out[...] = jnp.zeros_like(out)
    row = lax.broadcasted_iota(jnp.int32, (HALF, HALF), 0)
    lane = lax.broadcasted_iota(jnp.int32, (HALF, HALF), 1)
    for window in range(6):
        side, position = window // 2, window % 2
        column = near_offs[side, position, 1] if side < 2 else offs[position, 1]
        block, shift = column_block(column, width)
        base = block * HALF
        value = grads[0, window, 0]
        if side == 0:
            value = jnp.where(jnp.concatenate([row, row], 1) < near_offs[0, position, 0], value, 0.0)
        elif side == 1:
            value = jnp.where(jnp.concatenate([row, row], 1) >= near_offs[1, position, 0], value, 0.0)
        mixed, pure = value[:, :HALF], value[:, HALF:]
        first = lane >= shift
        out[0, 0, :, pl.ds(pl.multiple_of(base, HALF), HALF)] += jnp.where(first, mixed, 0.0)
        out[0, 0, :, pl.ds(pl.multiple_of(base + HALF, HALF), HALF)] += pure
        out[0, 0, :, pl.ds(pl.multiple_of(base + 2 * HALF, HALF), HALF)] += jnp.where(first, 0.0, mixed)


def local(tiles, specimen, scan_offsets, probe_wave, fresnel_phase, measured):
    width = specimen.shape[3]
    any_space = pl.BlockSpec(memory_space=pl.ANY)
    smem = pl.BlockSpec(memory_space=pltpu.SMEM)
    dma = pltpu.SemaphoreType.DMA
    vm = lambda *shape: pltpu.VMEM(shape, F32)
    grads, near_offs = pl.pallas_call(
        functools.partial(main_kernel, tiles, width),
        out_shape=[
            jax.ShapeDtypeStruct((2, 6, 2, HALF, FULL), F32),
            jax.ShapeDtypeStruct((2, 2, 2), jnp.int32),
        ],
        in_specs=[smem] + [any_space] * 6,
        out_specs=[any_space, smem],
        scratch_shapes=[
            vm(2, 2, width // HALF, HALF, HALF),
            vm(2, FULL, FULL),
            vm(FULL, FULL),
            vm(FULL, FULL),
            pltpu.VMEM((4, 2, FULL, FULL), BF16),
            pltpu.VMEM((2, FULL, FULL), BF16),
            vm(2, 2, 2, 2, HALF, FULL),
            vm(2, 4, 2, HALF, FULL),
            vm(2, 2, HALF, FULL),
            vm(4, 2, HALF, FULL),
            vm(4, 2, FULL, FULL),
            vm(8, 2, FULL, FULL),
            vm(2, FULL, FULL),
            vm(2, FULL, FULL),
            vm(2, FULL, FULL),
            vm(4, 2, FULL, FULL),
            pltpu.SMEM((2, 2, 2), jnp.int32),
            dma((width // HALF,)), dma((5,)),
            dma((2,)), dma((2,)),
            dma((2, 2, 2)), dma((2, 4)),
            dma((2,)), dma((2,)),
            dma((2, 4)), dma((2, 4)),
            dma((2,)), dma((2,)), dma((2,)),
        ],
        compiler_params=pltpu.CompilerParams(
            collective_id=0, has_side_effects=True, vmem_limit_bytes=48 * 2**20
        ),
        name="ptycho",
    )(scan_offsets, specimen, probe_wave, fresnel_phase, measured, jnp.asarray(dft_tables()), jnp.asarray(order_tables()))
    return pl.pallas_call(
        functools.partial(place_kernel, width),
        out_shape=jax.ShapeDtypeStruct(specimen.shape, F32),
        grid=(2, 2),
        in_specs=[smem, smem, pl.BlockSpec((1, 6, 1, HALF, FULL), lambda s, c: (s, 0, c, 0, 0))],
        out_specs=pl.BlockSpec((1, 1, HALF, width), lambda s, c: (s, c, 0, 0)),
        name="place",
    )(scan_offsets, near_offs, grads)


def solution(mesh):
    placed = (P("depth", None, "tile", None), P("tile", None), P(), P(), P("tile", None, None))
    return jax.shard_map(
        functools.partial(local, mesh.shape["tile"]),
        mesh=mesh, in_specs=placed, out_specs=P("depth", None, "tile", None), check_vma=False,
    )
```

profile of v0, /device:TPU:6, one launch (start us, length us, event | category | flops | bytes accessed | tf_op | source)
XLA Modules:
  0.0 74.1 jit_solution(16255312722939663022)
XLA Ops:
  0.0 0.0 copy-start.1
  0.0 1.2 %copy-done.1 = bf16[4,2,256,256]{3,2,1,0:T(8,128)(2,1)S(1)} copy-done((bf16[4,2,256,256]{3,2,1,0:T(8,128)(2,1)S(1)}, bf16[4,2,256,256]{3,2,1,0:T(8,128)(2,1)}, u32[]{:S(2)}) %copy-start.1) | copy-done | bytes 1048600
  1.2 0.0 copy-start.2
  1.2 1.0 %copy-done.2 = f32[2,256,256]{2,1,0:T(8,128)S(1)} copy-done((f32[2,256,256]{2,1,0:T(8,128)S(1)}, f32[2,256,256]{2,1,0:T(8,128)}, u32[]{:S(2)}) %copy-start.2) | copy-done | bytes 524312
  2.3 0.0 copy-start.3
  2.3 1.0 %copy-done.3 = f32[2,256,256]{2,1,0:T(8,128)S(1)} copy-done((f32[2,256,256]{2,1,0:T(8,128)S(1)}, f32[2,256,256]{2,1,0:T(8,128)}, u32[]{:S(2)}) %copy-start.3) | copy-done | bytes 524312
  3.3 0.0 copy-start.4
  3.3 0.9 %copy-done.4 = f32[256,256]{1,0:T(8,128)S(1)} copy-done((f32[256,256]{1,0:T(8,128)S(1)}, f32[256,256]{1,0:T(8,128)}, u32[]{:S(2)}) %copy-start.4) | copy-done | bytes 262168
  4.3 0.0 copy-start.5
  4.3 0.9 %copy-done.5 = bf16[2,256,256]{2,1,0:T(8,128)(2,1)S(1)} copy-done((bf16[2,256,256]{2,1,0:T(8,128)(2,1)S(1)}, bf16[2,256,256]{2,1,0:T(8,128)(2,1)}, u32[]{:S(2)}) %copy-start.5) | copy-done | bytes 262168
  5.2 0.0 copy-start.6
  5.2 0.7 copy-done.6
  5.9 61.1 %ptycho.1 = (f32[2,6,2,128,256]{4,3,2,1,0:T(8,128)S(1)}, s32[2,2,2]{2,1,0:T(2,128)S(1)}) custom-call(s32[2,2]{1,0:T(2,128)S(1)} %copy-done.6, f32[2,2,128,2048]{3,2,1,0:T(8,128)} %spec_hbm.1, f32[2,256,256]{2,1,0:T(8,128)S(1)} %copy-done.2, f32[256,256]{1,0:T(8,128)S(1)} %copy-done.4, f32[2,256,256]{2,1,0:T(8,128)S(1)} %copy-done.3, ...), custom_call_target="tpu_custom_call" | custom-call | tf_op jit(solution)/shard_map/ptycho/pallas_call | solution.py:399
  67.0 0.0 copy-start
  67.0 1.6 %copy-done = f32[2,6,2,128,256]{4,3,2,1,0:T(8,128)} copy-done((f32[2,6,2,128,256]{4,3,2,1,0:T(8,128)}, f32[2,6,2,128,256]{4,3,2,1,0:T(8,128)S(1)}, u32[]{:S(2)}) %copy-start) | copy-done | bytes 3145752
  68.6 0.0 copy-start.7
  68.6 0.5 copy-done.7
  69.2 5.0 %place.1 = f32[2,2,128,2048]{3,2,1,0:T(8,128)} custom-call(s32[2,2]{1,0:T(2,128)} %offs.3, s32[2,2,2]{2,1,0:T(2,128)} %copy-done.7, f32[2,6,2,128,256]{4,3,2,1,0:T(8,128)} %copy-done), custom_call_target="tpu_custom_call" | custom-call | tf_op jit(solution)/shard_map/place/pallas_call | solution.py:437
Async XLA Ops:
  0.0 1.2 %copy-start.1 = (bf16[4,2,256,256]{3,2,1,0:T(8,128)(2,1)S(1)}, bf16[4,2,256,256]{3,2,1,0:T(8,128)(2,1)}, u32[]{:S(2)}) copy-start(bf16[4,2,256,256]{3,2,1,0:T(8,128)(2,1)} %constant.4.clone.tab_hbm) | copy-start | bytes 3145732
  1.2 1.0 %copy-start.2 = (f32[2,256,256]{2,1,0:T(8,128)S(1)}, f32[2,256,256]{2,1,0:T(8,128)}, u32[]{:S(2)}) copy-start(f32[2,256,256]{2,1,0:T(8,128)} %probe_hbm.1) | copy-start | bytes 1572868
  2.3 1.0 %copy-start.3 = (f32[2,256,256]{2,1,0:T(8,128)S(1)}, f32[2,256,256]{2,1,0:T(8,128)}, u32[]{:S(2)}) copy-start(f32[2,256,256]{2,1,0:T(8,128)} %meas_hbm.1) | copy-start | bytes 1572868
  3.3 0.9 %copy-start.4 = (f32[256,256]{1,0:T(8,128)S(1)}, f32[256,256]{1,0:T(8,128)}, u32[]{:S(2)}) copy-start(f32[256,256]{1,0:T(8,128)} %phase_hbm.1) | copy-start | bytes 786436
  4.3 0.9 %copy-start.5 = (bf16[2,256,256]{2,1,0:T(8,128)(2,1)S(1)}, bf16[2,256,256]{2,1,0:T(8,128)(2,1)}, u32[]{:S(2)}) copy-start(bf16[2,256,256]{2,1,0:T(8,128)(2,1)} %constant.5.clone.perm_hbm) | copy-start | bytes 786436
  5.2 0.7 copy-start.6
  67.0 1.6 %copy-start = (f32[2,6,2,128,256]{4,3,2,1,0:T(8,128)}, f32[2,6,2,128,256]{4,3,2,1,0:T(8,128)S(1)}, u32[]{:S(2)}) copy-start(f32[2,6,2,128,256]{4,3,2,1,0:T(8,128)S(1)} %get-tuple-element.8.grads) | copy-start | bytes 9437188
  68.6 0.5 copy-start.7
where the time goes:
time: 74.5 us; the launch traced here: 74.1 us
  Pallas kernels  66.1 us (89%)
  local copies, waits for them, and re-layouts  8.06 us (11%)
    pallas_call x1, Pallas kernels, local(): pl.pallas_call(functools.partial(main_kernel, tiles, width), out_shape=[j...  61.1 us
    unnamed x16, local copies, waits for them, and re-layouts  8.06 us
    pallas_call x1, Pallas kernels, local(): pl.pallas_call(functools.partial(place_kernel, width), out_shape=jax.Shap...  4.96 us

commit v1 on v0

--- a/solution.py
+++ b/solution.py
@@ -119,11 +119,11 @@
 
 def main_kernel(
     tiles, width,
-    offs, spec_hbm, probe_hbm, phase_hbm, meas_hbm, tab_hbm, perm_hbm,
+    offs_hbm, spec_hbm, probe_hbm, phase_hbm, meas_hbm, tab_hbm, perm_hbm,
     grads, offs_out,
-    spec, probe, phase, meas, tab, perm,
+    offs, offs_table, spec, probe, phase, meas, tab, perm,
     staged, near, own_staged, own, patch, field, x_buf, z_buf, kern, update, offs_land,
-    block_sem, load_sem, off_send, off_recv, in_send, in_recv, sib_send, sib_recv,
+    offs_sem, block_sem, load_sem, off_send, off_recv, in_send, in_recv, sib_send, sib_recv,
     out_send, out_recv, mid_send, mid_recv, mid_local,
 ):
     me = lax.axis_index("tile")
@@ -161,10 +161,14 @@
         pltpu.make_async_copy(phase_hbm, phase, load_sem.at[3]),
         pltpu.make_async_copy(meas_hbm.at[core], meas, load_sem.at[4]),
     ]
+    offs_load = pltpu.make_async_copy(offs_hbm, offs, offs_sem.at[0])
+    offs_store = pltpu.make_async_copy(offs_table, offs_out, offs_sem.at[1])
+    offs_load.start()
     for b in range(blocks):
         block_copy(b).start()
     for copy in loads:
         copy.start()
+    offs_load.wait()
     pl.semaphore_wait(barrier, 1 + 2 * has_above.astype(jnp.int32) + 2 * has_below.astype(jnp.int32))
 
     def offsets_copy(side):
@@ -228,8 +232,12 @@
     for side, there in sides:
         for position in (0, 1):
             first = offs_land[side, position, 0] - (me - 2 + 2 * side) * HALF
-            offs_out[side, position, 0] = jnp.where(there, first, HALF * side)
-            offs_out[side, position, 1] = jnp.where(there, offs_land[side, position, 1], 0)
+            offs_table[side, position, 0] = jnp.where(there, first, HALF * side)
+            offs_table[side, position, 1] = jnp.where(there, offs_land[side, position, 1], 0)
+    for position in (0, 1):
+        offs_table[2, position, 0] = 0
+        offs_table[2, position, 1] = offs[position, 1]
+    offs_store.start()
 
     first = offs[core, 0] - (me - 1) * HALF
     unused, shift = column_block(offs[core, 1], width)
@@ -343,6 +351,7 @@
 
     lax.fori_loop(0, 7, step, 0)
 
+    offs_store.wait()
     for layer in (0, 1):
         middle_local(layer).wait()
         middle_copy(layer).wait_send()
@@ -369,42 +378,58 @@
                     ).wait_recv()
 
 
-def place_kernel(width, offs, near_offs, grads, out):
-    out[...] = jnp.zeros_like(out)
-    row = lax.broadcasted_iota(jnp.int32, (HALF, HALF), 0)
+def place_kernel(width, offs_hbm, grads, out, offs, held, strip, offs_sem, in_sem, out_sem):
+    def in_copy(layer, c):
+        return pltpu.make_async_copy(grads.at[layer, :, c], held.at[layer, c], in_sem.at[layer, c])
+
+    def out_copy(layer, c):
+        return pltpu.make_async_copy(strip.at[layer, c], out.at[layer, c], out_sem.at[layer, c])
+
+    parts = [(layer, c) for layer in (0, 1) for c in (0, 1)]
+    offs_load = pltpu.make_async_copy(offs_hbm, offs, offs_sem)
+    offs_load.start()
+    for part in parts:
+        in_copy(*part).start()
+    strip[...] = jnp.zeros_like(strip)
+    row = lax.broadcasted_iota(jnp.int32, (HALF, FULL), 0)
     lane = lax.broadcasted_iota(jnp.int32, (HALF, HALF), 1)
-    for window in range(6):
-        side, position = window // 2, window % 2
-        column = near_offs[side, position, 1] if side < 2 else offs[position, 1]
-        block, shift = column_block(column, width)
-        base = block * HALF
-        value = grads[0, window, 0]
-        if side == 0:
-            value = jnp.where(jnp.concatenate([row, row], 1) < near_offs[0, position, 0], value, 0.0)
-        elif side == 1:
-            value = jnp.where(jnp.concatenate([row, row], 1) >= near_offs[1, position, 0], value, 0.0)
-        mixed, pure = value[:, :HALF], value[:, HALF:]
-        first = lane >= shift
-        out[0, 0, :, pl.ds(pl.multiple_of(base, HALF), HALF)] += jnp.where(first, mixed, 0.0)
-        out[0, 0, :, pl.ds(pl.multiple_of(base + HALF, HALF), HALF)] += pure
-        out[0, 0, :, pl.ds(pl.multiple_of(base + 2 * HALF, HALF), HALF)] += jnp.where(first, 0.0, mixed)
+    offs_load.wait()
+    for layer, c in parts:
+        in_copy(layer, c).wait()
+        for window in range(6):
+            side, position = window // 2, window % 2
+            block, shift = column_block(offs[side, position, 1], width)
+            value = held[layer, c, window]
+            if side == 0:
+                value = jnp.where(row < offs[0, position, 0], value, 0.0)
+            elif side == 1:
+                value = jnp.where(row >= offs[1, position, 0], value, 0.0)
+            mixed, pure = value[:, :HALF], value[:, HALF:]
+            first = lane >= shift
+            for k, piece in enumerate((jnp.where(first, mixed, 0.0), pure, jnp.where(first, 0.0, mixed))):
+                span = pl.ds(pl.multiple_of((block + k) * HALF, HALF), HALF)
+                strip[layer, c, :, span] += piece
+        out_copy(layer, c).start()
+    for part in parts:
+        out_copy(*part).wait()
 
 
 def local(tiles, specimen, scan_offsets, probe_wave, fresnel_phase, measured):
     width = specimen.shape[3]
     any_space = pl.BlockSpec(memory_space=pl.ANY)
-    smem = pl.BlockSpec(memory_space=pltpu.SMEM)
     dma = pltpu.SemaphoreType.DMA
     vm = lambda *shape: pltpu.VMEM(shape, F32)
     grads, near_offs = pl.pallas_call(
         functools.partial(main_kernel, tiles, width),
         out_shape=[
             jax.ShapeDtypeStruct((2, 6, 2, HALF, FULL), F32),
-            jax.ShapeDtypeStruct((2, 2, 2), jnp.int32),
+            jax.ShapeDtypeStruct((3, 2, 2), jnp.int32),
         ],
-        in_specs=[smem] + [any_space] * 6,
-        out_specs=[any_space, smem],
+        in_specs=[any_space] * 7,
+        out_specs=[any_space, any_space],
         scratch_shapes=[
+            pltpu.SMEM((2, 2), jnp.int32),
+            pltpu.SMEM((3, 2, 2), jnp.int32),
             vm(2, 2, width // HALF, HALF, HALF),
             vm(2, FULL, FULL),
             vm(FULL, FULL),
@@ -422,7 +447,7 @@
             vm(2, FULL, FULL),
             vm(4, 2, FULL, FULL),
             pltpu.SMEM((2, 2, 2), jnp.int32),
-            dma((width // HALF,)), dma((5,)),
+            dma((2,)), dma((width // HALF,)), dma((5,)),
             dma((2,)), dma((2,)),
             dma((2, 2, 2)), dma((2, 4)),
             dma((2,)), dma((2,)),
@@ -430,18 +455,22 @@
             dma((2,)), dma((2,)), dma((2,)),
         ],
         compiler_params=pltpu.CompilerParams(
-            collective_id=0, has_side_effects=True, vmem_limit_bytes=48 * 2**20
+            collective_id=0, has_side_effects=True, vmem_limit_bytes=60 * 2**20
         ),
         name="ptycho",
     )(scan_offsets, specimen, probe_wave, fresnel_phase, measured, jnp.asarray(dft_tables()), jnp.asarray(order_tables()))
     return pl.pallas_call(
         functools.partial(place_kernel, width),
         out_shape=jax.ShapeDtypeStruct(specimen.shape, F32),
-        grid=(2, 2),
-        in_specs=[smem, smem, pl.BlockSpec((1, 6, 1, HALF, FULL), lambda s, c: (s, 0, c, 0, 0))],
-        out_specs=pl.BlockSpec((1, 1, HALF, width), lambda s, c: (s, c, 0, 0)),
+        in_specs=[any_space, any_space],
+        out_specs=any_space,
+        scratch_shapes=[
+            pltpu.SMEM((3, 2, 2), jnp.int32), vm(2, 2, 6, HALF, FULL), vm(2, 2, HALF, width),
+            dma, dma((2, 2)), dma((2, 2)),
+        ],
+        compiler_params=pltpu.CompilerParams(vmem_limit_bytes=60 * 2**20),
         name="place",
-    )(scan_offsets, near_offs, grads)
+    )(near_offs, grads)
 
 
 def solution(mesh):

time: 74.5 us -> 63.6 us (0.85)
  local copies, waits for them, and re-layouts: 8.06 us -> 0 us
  Pallas kernels: 66.1 us -> 63.5 us
    unnamed x16 -> x0, local copies, waits for them, and re-layouts: 8.06 us -> none
    pallas_call x1, Pallas kernels: 4.96 us -> 3.46 us  [local(): pl.pallas_call(functools.partial(place_kernel, width), out_shape=jax.Shap...]
    pallas_call x1, Pallas kernels: 61.1 us -> 60 us  [local(): pl.pallas_call(functools.partial(main_kernel, tiles, width), out_shape=[j...]
where the time goes in v1:
time: 63.6 us; the launch traced here: 63.5 us
  Pallas kernels  63.5 us (100%)
    pallas_call x1, Pallas kernels, local(): pl.pallas_call(functools.partial(main_kernel, tiles, width), out_shape=[j...  60 us
    pallas_call x1, Pallas kernels, local(): pl.pallas_call(functools.partial(place_kernel, width), out_shape=jax.Shap...  3.46 us

profile of v1, /device:TPU:6, one launch (start us, length us, event | category | flops | bytes accessed | tf_op | source)
XLA Modules:
  0.0 63.5 jit_solution(15776298684245205970)
XLA Ops:
  0.0 60.0 %ptycho.1 = (f32[2,6,2,128,256]{4,3,2,1,0:T(8,128)}, s32[3,2,2]{2,1,0:T(2,128)}) custom-call(s32[2,2]{1,0:T(2,128)} %offs_hbm.1, f32[2,2,128,2048]{3,2,1,0:T(8,128)} %spec_hbm.1, f32[2,256,256]{2,1,0:T(8,128)} %probe_hbm.1, f32[256,256]{1,0:T(8,128)} %phase_hbm.1, f32[2,256,256]{2,1,0:T(8,128)} %meas_hbm.1, bf16[4,2,256,256]{3,2,1,0:T(8,128)(2,1)} %constant.4.clone.tab_hbm, ...), custom_call_target="tpu_custom_call" | custom-call | tf_op jit(solution)/shard_map/ptycho/pallas_call | solution.py:422
  60.0 3.5 %place.1 = f32[2,2,128,2048]{3,2,1,0:T(8,128)} custom-call(s32[3,2,2]{2,1,0:T(2,128)} %get-tuple-element.7.offs_hbm, f32[2,6,2,128,256]{4,3,2,1,0:T(8,128)} %get-tuple-element.8.grads), custom_call_target="tpu_custom_call" | custom-call | tf_op jit(solution)/shard_map/place/pallas_call | solution.py:462

commit v2 on v1

--- a/solution.py
+++ b/solution.py
@@ -14,6 +14,7 @@
 BF16 = jnp.bfloat16
 HALF = 128
 FULL = 256
+RING = 4
 
 
 def halves(matrix):
@@ -122,9 +123,9 @@
     offs_hbm, spec_hbm, probe_hbm, phase_hbm, meas_hbm, tab_hbm, perm_hbm,
     grads, offs_out,
     offs, offs_table, spec, probe, phase, meas, tab, perm,
-    staged, near, own_staged, own, patch, field, x_buf, z_buf, kern, update, offs_land,
+    staged, near, own_staged, own, patch, field, x_buf, z_buf, kern, update, relayed, offs_land,
     offs_sem, block_sem, load_sem, off_send, off_recv, in_send, in_recv, sib_send, sib_recv,
-    out_send, out_recv, mid_send, mid_recv, mid_local,
+    out_send, out_recv, mid_send, mid_recv, mid_local, relay_send, relay_recv, relay_ready,
 ):
     me = lax.axis_index("tile")
     core = lax.axis_index("depth")
@@ -134,6 +135,14 @@
     above = jnp.maximum(me - 1, 0)
     below = jnp.minimum(me + 1, tiles - 1)
 
+    place = lax.rem(me, RING * RING)
+    far_source = (place == RING * RING - 1) & has_below & (core == 1)
+    relays = (place == RING * RING - 3) & (me + 3 < tiles) & (core == 1)
+    far_target = (place == 0) & has_above & (core == 1)
+
+    def tile_at(distance):
+        return jnp.clip(me + distance, 0, tiles - 1)
+
     barrier = pltpu.get_barrier_semaphore()
     pl.semaphore_signal(barrier, inc=1, device_id=(other, me), device_id_type=MESH)
 
@@ -146,6 +155,11 @@
     def _():
         for d in (0, 1):
             pl.semaphore_signal(barrier, inc=1, device_id=(d, below), device_id_type=MESH)
+
+    @pl.when(relays)
+    def _():
+        pl.semaphore_signal(barrier, inc=1, device_id=(core, tile_at(2)), device_id_type=MESH)
+        pl.semaphore_signal(barrier, inc=1, device_id=(core, tile_at(3)), device_id_type=MESH)
 
     blocks = width // HALF
 
@@ -169,7 +183,8 @@
     for copy in loads:
         copy.start()
     offs_load.wait()
-    pl.semaphore_wait(barrier, 1 + 2 * has_above.astype(jnp.int32) + 2 * has_below.astype(jnp.int32))
+    present = 1 + 2 * has_above.astype(jnp.int32) + 2 * has_below.astype(jnp.int32)
+    pl.semaphore_wait(barrier, present + (far_source | far_target).astype(jnp.int32))
 
     def offsets_copy(side):
         return pltpu.make_async_remote_copy(
@@ -180,6 +195,10 @@
     sides = ((0, has_above), (1, has_below))
     for side, there in sides:
         pl.when(there)(offsets_copy(side).start)
+
+    @pl.when(far_target)
+    def _():
+        pl.semaphore_signal(relay_ready, inc=1, device_id=(core, tile_at(-3)), device_id_type=MESH)
 
     for b in range(blocks):
         block_copy(b).wait()
@@ -210,24 +229,56 @@
             device_id=(position, above if side == 0 else below), device_id_type=MESH,
         )
 
-    for side, there in sides:
-        @pl.when(there)
-        def _(side=side):
-            pltpu.make_async_remote_copy(
-                src_ref=offs, dst_ref=offs_land.at[side], send_sem=off_send.at[side], recv_sem=off_recv.at[side],
-                device_id=(core, above if side == 0 else below), device_id_type=MESH,
-            ).wait_recv()
-
-    for position in (0, 1):
-        for layer in (0, 1):
-            for side, there in sides:
-                @pl.when(there)
-                def _(position=position, layer=layer, side=side):
-                    for c in (0, 1):
-                        mixed, pure = take_window(spec, layer, c, offs_land[side, position, 1], width)
-                        staged[side, position, layer, c, :, :HALF] = mixed
-                        staged[side, position, layer, c, :, HALF:] = pure
-                    window_copy(position, layer, side).start()
+    def detour_copy():
+        return pltpu.make_async_remote_copy(
+            src_ref=staged.at[1, 1, 1], dst_ref=relayed, send_sem=in_send.at[1, 1, 1], recv_sem=relay_recv,
+            device_id=(core, tile_at(-2)), device_id_type=MESH,
+        )
+
+    def relay_copy():
+        return pltpu.make_async_remote_copy(
+            src_ref=relayed, dst_ref=near.at[0, 3], send_sem=relay_send, recv_sem=in_recv.at[0, 3],
+            device_id=(core, tile_at(3)), device_id_type=MESH,
+        )
+
+    def wait_offsets(side):
+        pltpu.make_async_remote_copy(
+            src_ref=offs, dst_ref=offs_land.at[side], send_sem=off_send.at[side], recv_sem=off_recv.at[side],
+            device_id=(core, above if side == 0 else below), device_id_type=MESH,
+        ).wait_recv()
+
+    def cut(side, position, layer):
+        for c in (0, 1):
+            mixed, pure = take_window(spec, layer, c, offs_land[side, position, 1], width)
+            staged[side, position, layer, c, :, :HALF] = mixed
+            staged[side, position, layer, c, :, HALF:] = pure
+
+    def send(side, position, layer):
+        cut(side, position, layer)
+        window_copy(position, layer, side).start()
+
+    def answer(side):
+        wait_offsets(side)
+        for position in (0, 1):
+            for layer in (0, 1):
+                send(side, position, layer)
+
+    first_of_ring = lax.rem(me, RING) == 0
+    usual = jnp.logical_not(far_source)
+    pl.when(has_above & jnp.logical_not(first_of_ring) & usual)(functools.partial(answer, 0))
+    pl.when(has_below & usual)(functools.partial(answer, 1))
+    pl.when(has_above & first_of_ring & usual)(functools.partial(answer, 0))
+
+    @pl.when(far_source)
+    def _():
+        wait_offsets(0)
+        send(0, 0, 0)
+        send(0, 0, 1)
+        wait_offsets(1)
+        cut(1, 1, 1)
+        detour_copy().start()
+        for side, position, layer in ((1, 0, 0), (0, 1, 0), (1, 0, 1), (0, 1, 1), (1, 1, 0)):
+            send(side, position, layer)
 
     for side, there in sides:
         for position in (0, 1):
@@ -310,6 +361,15 @@
             x_buf[0] = pr * ar + pi * ai
             x_buf[1] = pr * ai - pi * ar
 
+        @pl.when(relays & (i == 1))
+        def _():
+            pl.semaphore_wait(relay_ready, 1)
+            pltpu.make_async_remote_copy(
+                src_ref=relayed, dst_ref=relayed, send_sem=relay_send, recv_sem=relay_recv,
+                device_id=(core, tile_at(2)), device_id_type=MESH,
+            ).wait_recv()
+            relay_copy().start()
+
         forward_transform(x_buf, z_buf, tab)
 
         @pl.when(i == 3)
@@ -352,6 +412,7 @@
     lax.fori_loop(0, 7, step, 0)
 
     offs_store.wait()
+    pl.when(relays)(relay_copy().wait_send)
     for layer in (0, 1):
         middle_local(layer).wait()
         middle_copy(layer).wait_send()
@@ -446,6 +507,7 @@
             vm(2, FULL, FULL),
             vm(2, FULL, FULL),
             vm(4, 2, FULL, FULL),
+            vm(2, HALF, FULL),
             pltpu.SMEM((2, 2, 2), jnp.int32),
             dma((2,)), dma((width // HALF,)), dma((5,)),
             dma((2,)), dma((2,)),
@@ -453,6 +515,7 @@
             dma((2,)), dma((2,)),
             dma((2, 4)), dma((2, 4)),
             dma((2,)), dma((2,)), dma((2,)),
+            dma, dma, pltpu.SemaphoreType.REGULAR,
         ],
         compiler_params=pltpu.CompilerParams(
             collective_id=0, has_side_effects=True, vmem_limit_bytes=60 * 2**20

time: 63.6 us -> 62.7 us (0.986)
  Pallas kernels: 63.5 us -> 62.5 us
    pallas_call x1, Pallas kernels: 60 us -> 59.1 us  [local(): pl.pallas_call(functools.partial(main_kernel, tiles, width), out_shape=[j...]
where the time goes in v2:
time: 62.7 us; the launch traced here: 62.5 us
  Pallas kernels  62.5 us (100%)
    pallas_call x1, Pallas kernels, local(): pl.pallas_call(functools.partial(main_kernel, tiles, width), out_shape=[j...  59.1 us
    pallas_call x1, Pallas kernels, local(): pl.pallas_call(functools.partial(place_kernel, width), out_shape=jax.Shap...  3.46 us

profile of v2, /device:TPU:6, one launch (start us, length us, event | category | flops | bytes accessed | tf_op | source)
XLA Modules:
  0.0 62.5 jit_solution(12919858884196091366)
XLA Ops:
  0.0 59.1 %ptycho.1 = (f32[2,6,2,128,256]{4,3,2,1,0:T(8,128)}, s32[3,2,2]{2,1,0:T(2,128)}) custom-call(s32[2,2]{1,0:T(2,128)} %offs_hbm.1, f32[2,2,128,2048]{3,2,1,0:T(8,128)} %spec_hbm.1, f32[2,256,256]{2,1,0:T(8,128)} %probe_hbm.1, f32[256,256]{1,0:T(8,128)} %phase_hbm.1, f32[2,256,256]{2,1,0:T(8,128)} %meas_hbm.1, bf16[4,2,256,256]{3,2,1,0:T(8,128)(2,1)} %constant.4.clone.tab_hbm, ...), custom_call_target="tpu_custom_call" | custom-call | tf_op jit(solution)/shard_map/ptycho/pallas_call | solution.py:483
  59.1 3.5 %place.1 = f32[2,2,128,2048]{3,2,1,0:T(8,128)} custom-call(s32[3,2,2]{2,1,0:T(2,128)} %get-tuple-element.7.offs_hbm, f32[2,6,2,128,256]{4,3,2,1,0:T(8,128)} %get-tuple-element.8.grads), custom_call_target="tpu_custom_call" | custom-call | tf_op jit(solution)/shard_map/place/pallas_call | solution.py:525

commit v3 on v2

--- a/solution.py
+++ b/solution.py
@@ -15,6 +15,7 @@
 HALF = 128
 FULL = 256
 RING = 4
+DETOURED = (1,)
 
 
 def halves(matrix):
@@ -135,13 +136,14 @@
     above = jnp.maximum(me - 1, 0)
     below = jnp.minimum(me + 1, tiles - 1)
 
-    place = lax.rem(me, RING * RING)
-    far_source = (place == RING * RING - 1) & has_below & (core == 1)
-    relays = (place == RING * RING - 3) & (me + 3 < tiles) & (core == 1)
+    row = RING * RING
+    ring_rows = tiles // row
+    place = lax.rem(me, row)
+    far_source = (place == row - 1) & has_below & (core == 1)
+    relays = (me == 0) & (core == 1)
+    middle = ring_rows - 2
+    passes_on = (me == middle * row - 1) & (core == 1)
     far_target = (place == 0) & has_above & (core == 1)
-
-    def tile_at(distance):
-        return jnp.clip(me + distance, 0, tiles - 1)
 
     barrier = pltpu.get_barrier_semaphore()
     pl.semaphore_signal(barrier, inc=1, device_id=(other, me), device_id_type=MESH)
@@ -158,8 +160,14 @@
 
     @pl.when(relays)
     def _():
-        pl.semaphore_signal(barrier, inc=1, device_id=(core, tile_at(2)), device_id_type=MESH)
-        pl.semaphore_signal(barrier, inc=1, device_id=(core, tile_at(3)), device_id_type=MESH)
+        for k in range(1, ring_rows):
+            pl.semaphore_signal(barrier, inc=1, device_id=(1, k * row), device_id_type=MESH)
+            if k <= middle:
+                pl.semaphore_signal(barrier, inc=1, device_id=(1, k * row - 1), device_id_type=MESH)
+
+    @pl.when(passes_on)
+    def _():
+        pl.semaphore_signal(barrier, inc=1, device_id=(1, (middle + 1) * row - 1), device_id_type=MESH)
 
     blocks = width // HALF
 
@@ -198,7 +206,7 @@
 
     @pl.when(far_target)
     def _():
-        pl.semaphore_signal(relay_ready, inc=1, device_id=(core, tile_at(-3)), device_id_type=MESH)
+        pl.semaphore_signal(relay_ready, inc=1, device_id=(1, 0), device_id_type=MESH)
 
     for b in range(blocks):
         block_copy(b).wait()
@@ -229,17 +237,31 @@
             device_id=(position, above if side == 0 else below), device_id_type=MESH,
         )
 
-    def detour_copy():
-        return pltpu.make_async_remote_copy(
-            src_ref=staged.at[1, 1, 1], dst_ref=relayed, send_sem=in_send.at[1, 1, 1], recv_sem=relay_recv,
-            device_id=(core, tile_at(-2)), device_id_type=MESH,
-        )
-
-    def relay_copy():
-        return pltpu.make_async_remote_copy(
-            src_ref=relayed, dst_ref=near.at[0, 3], send_sem=relay_send, recv_sem=in_recv.at[0, 3],
-            device_id=(core, tile_at(3)), device_id_type=MESH,
-        )
+    def detour_copy(layer):
+        k = me // row
+        return pltpu.make_async_remote_copy(
+            src_ref=staged.at[1, 1, layer], dst_ref=relayed.at[k, layer], send_sem=in_send.at[1, 1, layer],
+            recv_sem=relay_recv.at[k, layer], device_id=(1, jnp.where(k == middle, middle * row - 1, 0)),
+            device_id_type=MESH,
+        )
+
+    def onward_copy(layer):
+        return pltpu.make_async_remote_copy(
+            src_ref=relayed.at[middle, layer], dst_ref=relayed.at[middle, layer], send_sem=relay_send.at[middle, layer],
+            recv_sem=relay_recv.at[middle, layer], device_id=(1, 0), device_id_type=MESH,
+        )
+
+    def relay_copy(k, layer):
+        return pltpu.make_async_remote_copy(
+            src_ref=relayed.at[k, layer], dst_ref=near.at[0, 2 + layer], send_sem=relay_send.at[k, layer],
+            recv_sem=in_recv.at[0, 2 + layer], device_id=(1, (k + 1) * row), device_id_type=MESH,
+        )
+
+    def wait_relayed(k, layer):
+        pltpu.make_async_remote_copy(
+            src_ref=relayed.at[k, layer], dst_ref=relayed.at[k, layer], send_sem=relay_send.at[k, layer],
+            recv_sem=relay_recv.at[k, layer], device_id=(1, row), device_id_type=MESH,
+        ).wait_recv()
 
     def wait_offsets(side):
         pltpu.make_async_remote_copy(
@@ -276,7 +298,7 @@
         send(0, 0, 1)
         wait_offsets(1)
         cut(1, 1, 1)
-        detour_copy().start()
+        detour_copy(1).start()
         for side, position, layer in ((1, 0, 0), (0, 1, 0), (1, 0, 1), (0, 1, 1), (1, 1, 0)):
             send(side, position, layer)
 
@@ -361,14 +383,19 @@
             x_buf[0] = pr * ar + pi * ai
             x_buf[1] = pr * ai - pi * ar
 
+        @pl.when(passes_on & (i == 0))
+        def _():
+            for layer in DETOURED:
+                wait_relayed(middle, layer)
+                onward_copy(layer).start()
+
         @pl.when(relays & (i == 1))
         def _():
-            pl.semaphore_wait(relay_ready, 1)
-            pltpu.make_async_remote_copy(
-                src_ref=relayed, dst_ref=relayed, send_sem=relay_send, recv_sem=relay_recv,
-                device_id=(core, tile_at(2)), device_id_type=MESH,
-            ).wait_recv()
-            relay_copy().start()
+            pl.semaphore_wait(relay_ready, ring_rows - 1)
+            for k in range(ring_rows - 1):
+                for layer in DETOURED:
+                    wait_relayed(k, layer)
+                    relay_copy(k, layer).start()
 
         forward_transform(x_buf, z_buf, tab)
 
@@ -412,7 +439,11 @@
     lax.fori_loop(0, 7, step, 0)
 
     offs_store.wait()
-    pl.when(relays)(relay_copy().wait_send)
+    for k in range(ring_rows - 1):
+        for layer in DETOURED:
+            pl.when(relays)(relay_copy(k, layer).wait_send)
+    for layer in DETOURED:
+        pl.when(passes_on)(onward_copy(layer).wait_send)
     for layer in (0, 1):
         middle_local(layer).wait()
         middle_copy(layer).wait_send()
@@ -507,7 +538,7 @@
             vm(2, FULL, FULL),
             vm(2, FULL, FULL),
             vm(4, 2, FULL, FULL),
-            vm(2, HALF, FULL),
+            vm(tiles // (RING * RING) - 1, 2, 2, HALF, FULL),
             pltpu.SMEM((2, 2, 2), jnp.int32),
             dma((2,)), dma((width // HALF,)), dma((5,)),
             dma((2,)), dma((2,)),
@@ -515,7 +546,7 @@
             dma((2,)), dma((2,)),
             dma((2, 4)), dma((2, 4)),
             dma((2,)), dma((2,)), dma((2,)),
-            dma, dma, pltpu.SemaphoreType.REGULAR,
+            dma((tiles // (RING * RING) - 1, 2)), dma((tiles // (RING * RING) - 1, 2)), pltpu.SemaphoreType.REGULAR,
         ],
         compiler_params=pltpu.CompilerParams(
             collective_id=0, has_side_effects=True, vmem_limit_bytes=60 * 2**20

time: 62.7 us -> 61.9 us (0.987)
  Pallas kernels: 62.5 us -> 61.8 us
    pallas_call x1, Pallas kernels: 59.1 us -> 58.3 us  [local(): pl.pallas_call(functools.partial(main_kernel, tiles, width), out_shape=[j...]
where the time goes in v3:
time: 61.9 us; the launch traced here: 61.8 us
  Pallas kernels  61.8 us (100%)
    pallas_call x1, Pallas kernels, local(): pl.pallas_call(functools.partial(main_kernel, tiles, width), out_shape=[j...  58.3 us
    pallas_call x1, Pallas kernels, local(): pl.pallas_call(functools.partial(place_kernel, width), out_shape=jax.Shap...  3.46 us

profile of v3, /device:TPU:6, one launch (start us, length us, event | category | flops | bytes accessed | tf_op | source)
XLA Modules:
  0.0 61.8 jit_solution(6164615123199051400)
XLA Ops:
  0.0 58.3 %ptycho.1 = (f32[2,6,2,128,256]{4,3,2,1,0:T(8,128)}, s32[3,2,2]{2,1,0:T(2,128)}) custom-call(s32[2,2]{1,0:T(2,128)} %offs_hbm.1, f32[2,2,128,2048]{3,2,1,0:T(8,128)} %spec_hbm.1, f32[2,256,256]{2,1,0:T(8,128)} %probe_hbm.1, f32[256,256]{1,0:T(8,128)} %phase_hbm.1, f32[2,256,256]{2,1,0:T(8,128)} %meas_hbm.1, bf16[4,2,256,256]{3,2,1,0:T(8,128)(2,1)} %constant.4.clone.tab_hbm, ...), custom_call_target="tpu_custom_call" | custom-call | tf_op jit(solution)/shard_map/ptycho/pallas_call | solution.py:514
  58.4 3.5 %place.1 = f32[2,2,128,2048]{3,2,1,0:T(8,128)} custom-call(s32[3,2,2]{2,1,0:T(2,128)} %get-tuple-element.7.offs_hbm, f32[2,6,2,128,256]{4,3,2,1,0:T(8,128)} %get-tuple-element.8.grads), custom_call_target="tpu_custom_call" | custom-call | tf_op jit(solution)/shard_map/place/pallas_call | solution.py:556

commit v4 on v3

--- a/solution.py
+++ b/solution.py
@@ -153,10 +153,17 @@
         for d in (0, 1):
             pl.semaphore_signal(barrier, inc=1, device_id=(d, above), device_id_type=MESH)
 
+    row_starts = (place == 0) & has_above
+    row_ends = (place == row - 1) & has_below
+    early = row_starts & (core == 0)
+
     @pl.when(has_below)
     def _():
-        for d in (0, 1):
-            pl.semaphore_signal(barrier, inc=1, device_id=(d, below), device_id_type=MESH)
+        pl.semaphore_signal(barrier, inc=1, device_id=(1, below), device_id_type=MESH)
+
+    @pl.when(has_below & jnp.logical_not(row_ends))
+    def _():
+        pl.semaphore_signal(barrier, inc=1, device_id=(0, below), device_id_type=MESH)
 
     @pl.when(relays)
     def _():
@@ -192,7 +199,8 @@
         copy.start()
     offs_load.wait()
     present = 1 + 2 * has_above.astype(jnp.int32) + 2 * has_below.astype(jnp.int32)
-    pl.semaphore_wait(barrier, present + (far_source | far_target).astype(jnp.int32))
+    present += (far_source | far_target).astype(jnp.int32) - 2 * early.astype(jnp.int32)
+    pl.semaphore_wait(barrier, present)
 
     def offsets_copy(side):
         return pltpu.make_async_remote_copy(
@@ -201,8 +209,15 @@
         )
 
     sides = ((0, has_above), (1, has_below))
-    for side, there in sides:
-        pl.when(there)(offsets_copy(side).start)
+    def offsets_across():
+        return pltpu.make_async_remote_copy(
+            src_ref=offs, dst_ref=offs_land.at[1], send_sem=off_send.at[2], recv_sem=off_recv.at[1],
+            device_id=(0, above), device_id_type=MESH,
+        )
+
+    pl.when(has_above & jnp.logical_not(early))(offsets_copy(0).start)
+    pl.when(has_below)(offsets_copy(1).start)
+    pl.when(row_starts & (core == 1))(offsets_across().start)
 
     @pl.when(far_target)
     def _():
@@ -279,28 +294,25 @@
         cut(side, position, layer)
         window_copy(position, layer, side).start()
 
-    def answer(side):
-        wait_offsets(side)
+    def answer(near_side):
+        far_side = 1 - near_side
         for position in (0, 1):
-            for layer in (0, 1):
-                send(side, position, layer)
+            for side in (near_side, far_side):
+                @pl.when(sides[side][1])
+                def _(position=position, side=side):
+                    if position == 0:
+                        wait_offsets(side)
+                    for layer in (0, 1):
+                        if near_side == 0 and side == 1 and position == 1 and layer == 1:
+                            cut(side, position, layer)
+                            pl.when(far_source)(detour_copy(layer).start)
+                            pl.when(jnp.logical_not(far_source))(window_copy(position, layer, side).start)
+                        else:
+                            send(side, position, layer)
 
     first_of_ring = lax.rem(me, RING) == 0
-    usual = jnp.logical_not(far_source)
-    pl.when(has_above & jnp.logical_not(first_of_ring) & usual)(functools.partial(answer, 0))
-    pl.when(has_below & usual)(functools.partial(answer, 1))
-    pl.when(has_above & first_of_ring & usual)(functools.partial(answer, 0))
-
-    @pl.when(far_source)
-    def _():
-        wait_offsets(0)
-        send(0, 0, 0)
-        send(0, 0, 1)
-        wait_offsets(1)
-        cut(1, 1, 1)
-        detour_copy(1).start()
-        for side, position, layer in ((1, 0, 0), (0, 1, 0), (1, 0, 1), (0, 1, 1), (1, 1, 0)):
-            send(side, position, layer)
+    pl.when(first_of_ring)(functools.partial(answer, 1))
+    pl.when(jnp.logical_not(first_of_ring))(functools.partial(answer, 0))
 
     for side, there in sides:
         for position in (0, 1):
@@ -444,6 +456,9 @@
             pl.when(relays)(relay_copy(k, layer).wait_send)
     for layer in DETOURED:
         pl.when(passes_on)(onward_copy(layer).wait_send)
+    pl.when(has_above & jnp.logical_not(early))(offsets_copy(0).wait_send)
+    pl.when(has_below)(offsets_copy(1).wait_send)
+    pl.when(row_starts & (core == 1))(offsets_across().wait_send)
     for layer in (0, 1):
         middle_local(layer).wait()
         middle_copy(layer).wait_send()
@@ -455,7 +470,6 @@
     for side, there in sides:
         @pl.when(there)
         def _(side=side):
-            offsets_copy(side).wait_send()
             for position in (0, 1):
                 for layer in (0, 1):
                     window_copy(position, layer, side).wait_send()
@@ -541,7 +555,7 @@
             vm(tiles // (RING * RING) - 1, 2, 2, HALF, FULL),
             pltpu.SMEM((2, 2, 2), jnp.int32),
             dma((2,)), dma((width // HALF,)), dma((5,)),
-            dma((2,)), dma((2,)),
+            dma((3,)), dma((2,)),
             dma((2, 2, 2)), dma((2, 4)),
             dma((2,)), dma((2,)),
             dma((2, 4)), dma((2, 4)),

time: 61.9 us -> 61.9 us (level)
  no operation moved by 1% of the time
where the time goes in v4:
time: 61.9 us; the launch traced here: 61.8 us
  Pallas kernels  61.8 us (100%)
    pallas_call x1, Pallas kernels, local(): pl.pallas_call(functools.partial(main_kernel, tiles, width), out_shape=[j...  58.3 us
    pallas_call x1, Pallas kernels, local(): pl.pallas_call(functools.partial(place_kernel, width), out_shape=jax.Shap...  3.47 us

profile of v4, /device:TPU:6, one launch (start us, length us, event | category | flops | bytes accessed | tf_op | source)
XLA Modules:
  0.0 61.8 jit_solution(16350422536229157571)
XLA Ops:
  0.0 58.3 %ptycho.1 = (f32[2,6,2,128,256]{4,3,2,1,0:T(8,128)}, s32[3,2,2]{2,1,0:T(2,128)}) custom-call(s32[2,2]{1,0:T(2,128)} %offs_hbm.1, f32[2,2,128,2048]{3,2,1,0:T(8,128)} %spec_hbm.1, f32[2,256,256]{2,1,0:T(8,128)} %probe_hbm.1, f32[256,256]{1,0:T(8,128)} %phase_hbm.1, f32[2,256,256]{2,1,0:T(8,128)} %meas_hbm.1, bf16[4,2,256,256]{3,2,1,0:T(8,128)(2,1)} %constant.4.clone.tab_hbm, ...), custom_call_target="tpu_custom_call" | custom-call | tf_op jit(solution)/shard_map/ptycho/pallas_call | solution.py:528
  58.3 3.5 %place.1 = f32[2,2,128,2048]{3,2,1,0:T(8,128)} custom-call(s32[3,2,2]{2,1,0:T(2,128)} %get-tuple-element.7.offs_hbm, f32[2,6,2,128,256]{4,3,2,1,0:T(8,128)} %get-tuple-element.8.grads), custom_call_target="tpu_custom_call" | custom-call | tf_op jit(solution)/shard_map/place/pallas_call | solution.py:570

commit v5 on v4

--- a/solution.py
+++ b/solution.py
@@ -124,9 +124,9 @@
     offs_hbm, spec_hbm, probe_hbm, phase_hbm, meas_hbm, tab_hbm, perm_hbm,
     grads, offs_out,
     offs, offs_table, spec, probe, phase, meas, tab, perm,
-    staged, near, own_staged, own, patch, field, x_buf, z_buf, kern, update, relayed, offs_land,
+    staged, near, own_staged, own, patch, field, x_buf, z_buf, kern, update, relayed, back, offs_land,
     offs_sem, block_sem, load_sem, off_send, off_recv, in_send, in_recv, sib_send, sib_recv,
-    out_send, out_recv, mid_send, mid_recv, mid_local, relay_send, relay_recv, relay_ready,
+    out_send, out_recv, mid_send, mid_recv, mid_local, relay_send, relay_recv, back_send, back_recv, relay_ready,
 ):
     me = lax.axis_index("tile")
     core = lax.axis_index("depth")
@@ -164,6 +164,15 @@
     @pl.when(has_below & jnp.logical_not(row_ends))
     def _():
         pl.semaphore_signal(barrier, inc=1, device_id=(0, below), device_id_type=MESH)
+
+    relays_back = (place == RING - 1) & (me > row) & (core == 1)
+    back_source = jnp.maximum(me - 3, 0)
+    back_target = jnp.maximum(me - 4, 0)
+
+    @pl.when(relays_back)
+    def _():
+        pl.semaphore_signal(barrier, inc=1, device_id=(1, back_source), device_id_type=MESH)
+        pl.semaphore_signal(barrier, inc=1, device_id=(1, back_target), device_id_type=MESH)
 
     @pl.when(relays)
     def _():
@@ -199,7 +208,7 @@
         copy.start()
     offs_load.wait()
     present = 1 + 2 * has_above.astype(jnp.int32) + 2 * has_below.astype(jnp.int32)
-    present += (far_source | far_target).astype(jnp.int32) - 2 * early.astype(jnp.int32)
+    present += 2 * (far_source | far_target).astype(jnp.int32) - 2 * early.astype(jnp.int32)
     pl.semaphore_wait(barrier, present)
 
     def offsets_copy(side):
@@ -222,6 +231,10 @@
     @pl.when(far_target)
     def _():
         pl.semaphore_signal(relay_ready, inc=1, device_id=(1, 0), device_id_type=MESH)
+
+    @pl.when(far_source)
+    def _():
+        pl.semaphore_signal(relay_ready, inc=1, device_id=(1, jnp.minimum(me + 4, tiles - 1)), device_id_type=MESH)
 
     for b in range(blocks):
         block_copy(b).wait()
@@ -293,6 +306,24 @@
     def send(side, position, layer):
         cut(side, position, layer)
         window_copy(position, layer, side).start()
+
+    def back_direct():
+        return pltpu.make_async_remote_copy(
+            src_ref=staged.at[0, 1, 1, 1], dst_ref=near.at[1, 3, 1], send_sem=in_send.at[0, 1, 1],
+            recv_sem=in_recv.at[1, 3], device_id=(1, above), device_id_type=MESH,
+        )
+
+    def back_detour():
+        return pltpu.make_async_remote_copy(
+            src_ref=staged.at[0, 1, 1, 0], dst_ref=back, send_sem=in_send.at[0, 1, 1], recv_sem=back_recv,
+            device_id=(1, jnp.minimum(me + 3, tiles - 1)), device_id_type=MESH,
+        )
+
+    def back_relay():
+        return pltpu.make_async_remote_copy(
+            src_ref=back, dst_ref=near.at[1, 3, 0], send_sem=back_send, recv_sem=in_recv.at[1, 3],
+            device_id=(1, back_target), device_id_type=MESH,
+        )
 
     def answer(near_side):
         far_side = 1 - near_side
@@ -307,8 +338,18 @@
                             cut(side, position, layer)
                             pl.when(far_source)(detour_copy(layer).start)
                             pl.when(jnp.logical_not(far_source))(window_copy(position, layer, side).start)
+                        elif near_side == 1 and side == 0 and position == 1 and layer == 1:
+                            @pl.when(jnp.logical_not(far_target))
+                            def _():
+                                send(0, 1, 1)
                         else:
                             send(side, position, layer)
+                    if near_side == 1 and side == 0 and position == 0:
+                        @pl.when(far_target)
+                        def _():
+                            cut(0, 1, 1)
+                            back_detour().start()
+                            back_direct().start()
 
     first_of_ring = lax.rem(me, RING) == 0
     pl.when(first_of_ring)(functools.partial(answer, 1))
@@ -401,6 +442,15 @@
                 wait_relayed(middle, layer)
                 onward_copy(layer).start()
 
+        @pl.when(relays_back & (i == 1))
+        def _():
+            pl.semaphore_wait(relay_ready, 1)
+            pltpu.make_async_remote_copy(
+                src_ref=back, dst_ref=back, send_sem=back_send, recv_sem=back_recv,
+                device_id=(1, back_source), device_id_type=MESH,
+            ).wait_recv()
+            back_relay().start()
+
         @pl.when(relays & (i == 1))
         def _():
             pl.semaphore_wait(relay_ready, ring_rows - 1)
@@ -459,6 +509,7 @@
     pl.when(has_above & jnp.logical_not(early))(offsets_copy(0).wait_send)
     pl.when(has_below)(offsets_copy(1).wait_send)
     pl.when(row_starts & (core == 1))(offsets_across().wait_send)
+    pl.when(relays_back)(back_relay().wait_send)
     for layer in (0, 1):
         middle_local(layer).wait()
         middle_copy(layer).wait_send()
@@ -553,6 +604,7 @@
             vm(2, FULL, FULL),
             vm(4, 2, FULL, FULL),
             vm(tiles // (RING * RING) - 1, 2, 2, HALF, FULL),
+            vm(HALF, FULL),
             pltpu.SMEM((2, 2, 2), jnp.int32),
             dma((2,)), dma((width // HALF,)), dma((5,)),
             dma((3,)), dma((2,)),
@@ -560,7 +612,8 @@
             dma((2,)), dma((2,)),
             dma((2, 4)), dma((2, 4)),
             dma((2,)), dma((2,)), dma((2,)),
-            dma((tiles // (RING * RING) - 1, 2)), dma((tiles // (RING * RING) - 1, 2)), pltpu.SemaphoreType.REGULAR,
+            dma((tiles // (RING * RING) - 1, 2)), dma((tiles // (RING * RING) - 1, 2)),
+            dma, dma, pltpu.SemaphoreType.REGULAR,
         ],
         compiler_params=pltpu.CompilerParams(
             collective_id=0, has_side_effects=True, vmem_limit_bytes=60 * 2**20

time: 61.9 us -> 62 us (level)
  no operation moved by 1% of the time
where the time goes in v5:
time: 62 us; the launch traced here: 61.8 us
  Pallas kernels  61.8 us (100%)
    pallas_call x1, Pallas kernels, local(): pl.pallas_call(functools.partial(main_kernel, tiles, width), out_shape=[j...  58.4 us
    pallas_call x1, Pallas kernels, local(): pl.pallas_call(functools.partial(place_kernel, width), out_shape=jax.Shap...  3.46 us

profile of v5, /device:TPU:6, one launch (start us, length us, event | category | flops | bytes accessed | tf_op | source)
XLA Modules:
  0.0 61.8 jit_solution(920562835804488186)
XLA Ops:
  0.0 58.4 %ptycho.1 = (f32[2,6,2,128,256]{4,3,2,1,0:T(8,128)}, s32[3,2,2]{2,1,0:T(2,128)}) custom-call(s32[2,2]{1,0:T(2,128)} %offs_hbm.1, f32[2,2,128,2048]{3,2,1,0:T(8,128)} %spec_hbm.1, f32[2,256,256]{2,1,0:T(8,128)} %probe_hbm.1, f32[256,256]{1,0:T(8,128)} %phase_hbm.1, f32[2,256,256]{2,1,0:T(8,128)} %meas_hbm.1, bf16[4,2,256,256]{3,2,1,0:T(8,128)(2,1)} %constant.4.clone.tab_hbm, ...), custom_call_target="tpu_custom_call" | custom-call | tf_op jit(solution)/shard_map/ptycho/pallas_call | solution.py:579
  58.4 3.5 %place.1 = f32[2,2,128,2048]{3,2,1,0:T(8,128)} custom-call(s32[3,2,2]{2,1,0:T(2,128)} %get-tuple-element.7.offs_hbm, f32[2,6,2,128,256]{4,3,2,1,0:T(8,128)} %get-tuple-element.8.grads), custom_call_target="tpu_custom_call" | custom-call | tf_op jit(solution)/shard_map/place/pallas_call | solution.py:623
